TPU v7x, 32 devices: a whole 2x2x4 slice. The times are simulated.
32 devices in a mesh: groups: 2 (over y), patch: 8 (over z, x), head: 2 (over core).
Axes of the slice: x: 2, y: 2, z: 4, core: 2. Of those that a mesh axis runs over, the one named last changes fastest.
Arguments:
- tokens: bfloat16 [2048, 1536], P(('groups', 'patch', 'head')), parts along dimension 0, may hold values from -6 to 6
- timestep: int32 [2], P('groups'), parts along dimension 0, may hold values from 0 to 27
- text_length: int32 [2], P('groups'), parts along dimension 0, may hold values from 128 to 512
- mod_table: float32 [28, 3, 1536], replicated, may hold values from -4 to 4
- w_qkv: bfloat16 [1536, 3, 1536], P(None, None, 'head'), may hold values from -0.15625 to 0.15625
- q_gain: float32 [128], replicated, may hold values from 0.8 to 2
- k_gain: float32 [128], replicated, may hold values from 0.8 to 2
- w_out: bfloat16 [1536, 1536], replicated, may hold values from -0.15625 to 0.15625
- stale_kv: bfloat16 [2, 2048, 1536], P(None, ('groups', 'patch'), 'head'), parts along dimension 1, may hold values from -6 to 6
Outputs:
- update: bfloat16 [2048, 1536], P(('groups', 'patch', 'head')), parts along dimension 0
- new_kv: bfloat16 [2, 2048, 1536], P(None, ('groups', 'patch'), 'head'), parts along dimension 1
There are 2 independent parts, one for each index of `groups`. A program takes and returns all parts, laid end to end along the dimension named above; an argument that names none is the same for every part. Nothing has to cross between parts.
All inputs are finite; a program needn't handle non-finite values.
Results may differ from a plain program's by a relative error of at most 0.0089.
The roundings to bfloat16 on the way count: a program that leaves them out, or rounds other values in their place, can miss the bound.
Values may be sent and summed in bfloat16 or wider, within the bound.
A program may use at most 128 MiB of HBM per device.

v0:
```python
import math

import jax
import jax.numpy as jnp
from jax import lax
from jax.sharding import PartitionSpec as P

HD = 128


epsilon = 1e-06


def rms_scaled(values, gain_vec):
    mean_square = jnp.mean(values * values, axis=-1, keepdims=True)
    return (values * lax.rsqrt(mean_square + epsilon) * gain_vec).astype(jnp.bfloat16)


def shards(tokens, timestep, text_length, mod_table, w_qkv, q_gain, k_gain, w_out, stale_kv):
    n_head = lax.axis_size("head")
    tok_dev = tokens.shape[0]
    patch_rows = tok_dev * n_head
    text_rows = 4 * tok_dev * n_head
    width_dev = w_qkv.shape[2]
    heads_dev = width_dev // HD
    inverse_root = 1.0 / math.sqrt(HD)
    modulation = lax.dynamic_index_in_dim(mod_table, timestep[0], 0, keepdims=False)
    shift_row, scale_row, gate_row = (modulation[0], modulation[1], modulation[2])
    widened = tokens.astype(jnp.float32)
    centred = widened - jnp.mean(widened, axis=-1, keepdims=True)
    variance = jnp.mean(centred * centred, axis=-1, keepdims=True)
    normed = (centred * lax.rsqrt(variance + epsilon) * (1.0 + scale_row) + shift_row).astype(
        jnp.bfloat16
    )
    w_local = w_qkv.reshape(w_qkv.shape[0], 3 * width_dev)
    mixed = jnp.dot(
        lax.all_gather(normed, "head", axis=0, tiled=True),
        w_local,
        preferred_element_type=jnp.float32,
    )
    mixed = mixed.reshape(patch_rows, 3, heads_dev, HD)
    queries = rms_scaled(mixed[:, 0], q_gain)
    fresh_keys = rms_scaled(mixed[:, 1], k_gain)
    fresh_values = mixed[:, 2].astype(jnp.bfloat16)
    new_kv = jnp.stack(
        [fresh_keys.reshape(patch_rows, width_dev), fresh_values.reshape(patch_rows, width_dev)]
    )
    own_first = lax.axis_index("patch") * patch_rows
    length_limit = text_length[0]

    def attend_block(key_rows, value_rows, first_row, exclude_own):
        row_count = key_rows.shape[0]
        position = first_row + jnp.arange(row_count, dtype=jnp.int32)
        visible = (position >= text_rows) | (position < length_limit)
        if exclude_own:
            visible = visible & ((position < own_first) | (position >= own_first + patch_rows))
        scores = (
            jnp.einsum("qhd,khd->hqk", queries, key_rows, preferred_element_type=jnp.float32)
            * inverse_root
        )
        exps = jnp.exp(scores) * visible.astype(jnp.float32)[None, None, :]
        denominator = jnp.sum(exps, axis=-1)
        numerator = jnp.einsum(
            "hqk,khd->qhd",
            exps.astype(jnp.bfloat16),
            value_rows,
            preferred_element_type=jnp.float32,
        )
        return (numerator, denominator)

    fresh_num, fresh_den = attend_block(fresh_keys, fresh_values, own_first, False)
    gathered = lax.all_gather(stale_kv, "patch", axis=1, tiled=True)
    all_rows = gathered.shape[1]
    stale_num, stale_den = attend_block(
        gathered[0].reshape(all_rows, heads_dev, HD),
        gathered[1].reshape(all_rows, heads_dev, HD),
        jnp.int32(0),
        True,
    )
    numerator = stale_num + fresh_num
    denominator = stale_den + fresh_den
    attention = (
        (numerator / jnp.transpose(denominator)[:, :, None])
        .astype(jnp.bfloat16)
        .reshape(patch_rows, width_dev)
    )
    w_rows = lax.dynamic_slice_in_dim(w_out, lax.axis_index("head") * width_dev, width_dev, 0)
    projected = lax.psum_scatter(
        jnp.dot(attention, w_rows, preferred_element_type=jnp.float32),
        "head",
        scatter_dimension=0,
        tiled=True,
    )
    update = (gate_row * projected).astype(jnp.bfloat16)
    return (update, new_kv)


def solution(mesh):
    return jax.shard_map(
        shards,
        mesh=mesh,
        in_specs=(
            P(("groups", "patch", "head"), None),
            P("groups"),
            P("groups"),
            P(),
            P(None, None, "head"),
            P(),
            P(),
            P(),
            P(None, ("groups", "patch"), "head"),
        ),
        out_specs=(P(("groups", "patch", "head"), None), P(None, ("groups", "patch"), "head")),
        check_vma=False,
    )
```

profile of v0, /device:TPU:0, one launch (start us, length us, event | category | flops | bytes accessed | tf_op | source)
XLA Modules:
  0.0 97.5 jit_solution(3941530609824514863)
XLA Ops:
  7.2 0.0 all-gather.2.cloned.1.call-start
  7.2 1.9 %copy.20 = bf16[2,128,768]{1,2,0:T(8,128)(2,1)} copy(bf16[2,128,768]{2,1,0:T(8,128)(2,1)} %param.17) | data formatting | bytes 786432 | tf_op args[8]
  9.1 0.0 all-gather.2.cloned.1.call-update
  9.1 0.0 reduce-scatter.2.cloned.1.call-start
  9.9 0.0 copy-start
  9.9 10.3 %copy.19 = bf16[1536,3,768]{0,2,1:T(8,128)(2,1)} copy(bf16[1536,3,768]{2,0,1:T(8,128)(2,1)} %param.13) | data formatting | bytes 14155776 | tf_op args[4]
  20.9 0.9 dynamic-slice_reduce_fusion.1
  21.8 0.0 copy-done
  21.8 0.1 convert_reduce_fusion
  21.9 0.2 fusion.18
  22.2 0.2 fusion.21
  22.3 2.2 %all_gather.6 = bf16[128,1536]{1,0:T(8,128)(2,1)S(1)} all-gather(bf16[64,1536]{1,0:T(8,128)(2,1)S(1)} %fusion.21), channel_id=1, replica_groups=mesh['groups'=2,'patch'=8,'head'=2] {'head'}, dimensions={0}, use_global_device_ids=true | all-gather | bytes 589824 | tf_op jit(solution)/shard_map/all_gather | solution.py:37
  24.5 0.0 copy-start.1
  24.5 0.0 copy-start.2
  24.5 5.0 %fusion.22 = f32[128,3,6,128]{0,3,2,1:T(8,128)S(1)} fusion(bf16[3,6,128,1536]{3,2,1,0:T(8,128)(2,1)} %bitcast.69, bf16[128,1536]{1,0:T(8,128)(2,1)S(1)} %all_gather.6), kind=kOutput, calls=%fused_computation.27 | convolution fusion | flops 905969664 | bytes 8650752 | tf_op jit(solution)/shard_map/dot_general | solution.py:36
  29.5 0.1 fusion.24
  29.6 0.0 copy-done.1
  29.6 0.4 fusion.42
  30.0 46.4 %all-gather.2.cloned.1.call-done = bf16[2,1024,768]{1,2,0:T(8,128)(2,1)} async-done(((bf16[2,128,768]{1,2,0:T(8,128)(2,1)}), bf16[2,1024,768]{1,2,0:T(8,128)(2,1)}) %all-gather.2.cloned.1.call-update) | async-done | bytes 3145744 | tf_op jit(solution)/shard_map/all_gather | solution.py:72
  76.4 2.3 %fusion.41 = (bf16[1,1024,768]{1,2,0:T(8,128)(2,1)S(1)}, bf16[1,1024,768]{1,2,0:T(8,128)(2,1)S(1)}) fusion(bf16[2,1024,768]{1,2,0:T(8,128)(2,1)} %all-gather.2.cloned.1.call-done), kind=kLoop, calls=%fused_computation.65 | loop fusion | bytes 6291456 | tf_op jit(solution)/shard_map/slice | solution.py:75
  78.8 0.0 slice-start.1
  78.8 1.1 %fusion = (f32[6,128]{1,0:T(8,128)S(1)}, f32[6,128,1024]{2,1,0:T(8,128)S(1)}) fusion(f32[1024]{0:T(1024)S(1)} %fusion.35, bf16[1024,6,128]{0,2,1:T(8,128)(2,1)S(1)} %bitcast.71, f32[128,3,6,128]{0,3,2,1:T(8,128)S(1)} %fusion.22, f32[128]{0:T(128)S(1)} %copy-done.1, f32[128,6]{0,1:T(8,128)S(1)} %get-tuple-element.14), kind=kOutput, calls=%fused_computation.1 | convolution fusion | flops 203980032 | bytes 5123584 | tf_op jit(solution)/shard_map/qhd,khd->hqk/dot_general | solution.py:58
  79.9 0.8 fusion.10
  80.7 0.2 fusion.15
  81.0 1.4 %fusion.2 = f32[128,1536]{1,0:T(8,128)} fusion(bf16[128,768]{0,1:T(8,128)(2,1)S(1)} %bitcast.77, bf16[1536,1536]{1,0:T(8,128)(2,1)S(1)} %bitcast.75, s32[]{:T(128)S(6)} %select_n.8), kind=kOutput, calls=%fused_computation.3 | convolution fusion | flops 301989888 | bytes 3342340 | tf_op jit(solution)/shard_map/dot_general | solution.py:89
  82.3 0.0 reduce-scatter.2.cloned.1.call-update
  82.5 0.2 copy.27
  82.6 0.2 copy.26
  82.8 0.1 copy.28
  83.0 0.8 pad_maximum_fusion
  83.8 5.2 %reduce-scatter.2.cloned.1.call-done = f32[64,1536]{1,0:T(8,128)} async-done(((f32[128,1536]{1,0:T(8,128)}), f32[64,1536]{1,0:T(8,128)}) %reduce-scatter.2.cloned.1.call-update) | async-done | bytes 393232 | tf_op jit(solution)/shard_map/reduce_scatter | solution.py:88
  89.0 1.7 %multiply_convert_fusion.1 = bf16[64,1536]{1,0:T(8,128)(2,1)} fusion(f32[64,1536]{1,0:T(8,128)} %reduce-scatter.2.cloned.1.call-done, f32[1536]{0:T(1024)S(1)} %get-tuple-element.4), kind=kLoop, calls=%fused_computation.35 | loop fusion | flops 196608 | bytes 595968 | tf_op jit(solution)/shard_map/convert_element_type | solution.py:94
  (16 shorter events, 0.2 us)
Async XLA Ops:
  7.2 69.2 %all-gather.2.cloned.1.call-start = ((), (), s32[]{:S(2)}) async-start(), calls=%async_computation.1 | async-start | bytes 3538944 | tf_op jit(solution)/shard_map/all_gather | solution.py:72
  9.1 79.8 %reduce-scatter.2.cloned.1.call-start = ((), (), s32[]{:S(2)}) async-start(), calls=%async_computation.2 | async-start | bytes 1179648 | tf_op jit(solution)/shard_map/reduce_scatter | solution.py:88
  9.9 11.9 %copy-start = (bf16[64,1536]{1,0:T(8,128)(2,1)S(1)}, bf16[64,1536]{1,0:T(8,128)(2,1)}, u32[]{:S(2)}) copy-start(bf16[64,1536]{1,0:T(8,128)(2,1)} %param.9) | copy-start | bytes 589828
  24.5 5.1 %copy-start.1 = (f32[128]{0:T(128)S(1)}, f32[128]{0:T(128)}, u32[]{:S(2)}) copy-start(f32[128]{0:T(128)} %param.14) | copy-start | bytes 1540
  24.5 5.1 %copy-start.2 = (f32[128]{0:T(128)S(1)}, f32[128]{0:T(128)}, u32[]{:S(2)}) copy-start(f32[128]{0:T(128)} %param.15) | copy-start | bytes 1540
  76.4 4.5 %slice-start = ((s8[4718592]{0:T(1024)(128)(4,1)}), s8[4194304]{0:T(1024)(128)(4,1)S(1)}, s32[]{:S(2)}) async-start(s8[4718592]{0:T(1024)(128)(4,1)} %bitcast.74), calls=%async_computation.3 | async-start | bytes 8388608
  78.8 2.2 %slice-start.1 = ((s8[4718592]{0:T(1024)(128)(4,1)}), s8[524288]{0:T(1024)(128)(4,1)S(1)}, s32[]{:S(2)}) async-start(s8[4718592]{0:T(1024)(128)(4,1)} %bitcast.74), calls=%async_computation.4 | async-start | bytes 1048576
Sparse Core Ops, SparseCore 0:
  10.6 65.7 all-gather.1
  82.5 6.4 reduce-scatter.1
where the time goes:
time: 98 us; the launch traced here: 97.5 us
  waiting for transfers between devices  51.6 us (53%)
  between operations  15.6 us (16%)
  local copies, waits for them, and re-layouts  15.2 us (16%)
  matrix products  8.9 us (9%)
  other arithmetic  4.06 us (4%)
  blocking collectives  2.16 us (2%)
    all_gather x1, waiting for transfers between devices, shards(): gathered = lax.all_gather(stale_kv, 'patch', axis=1, tiled=True)  46.4 us
    unnamed x12, local copies, waits for them, and re-layouts  12.3 us
    reduce_scatter x1, waiting for transfers between devices, shards(): lax.psum_scatter(jnp.dot(attention, w_rows, preferred_element_type=jnp.fl...  5.16 us
    dot_general x1, matrix products, shards(): jnp.dot(lax.all_gather(normed, 'head', axis=0, tiled=True), w_local, pref...  5.01 us
    slice x1, local copies, waits for them, and re-layouts, shards(): gathered[0].reshape(all_rows, heads_dev, HD)  2.35 us
    all_gather x1, blocking collectives, shards(): lax.all_gather(normed, 'head', axis=0, tiled=True)  2.16 us
  transfers between devices with their start and end apart: 2, of which 2 were waited for; matrix products, arithmetic and copies ran while one was open for 19% of the time, Pallas kernels for 0%

commit v1 on v0

v1 whole, which is shorter than its diff:
```python
import math

import jax
import jax.numpy as jnp
from jax import lax
from jax.experimental import pallas as pl
from jax.experimental.pallas import tpu as pltpu
from jax.sharding import PartitionSpec as P

HD = 128
epsilon = 1e-06
MESH = pl.DeviceIdType.MESH
ACROSS, DOWN, UP = 0, 1, 2


def rms_scaled(values, gain_vec):
    mean_square = jnp.mean(values * values, axis=-1, keepdims=True)
    return (values * lax.rsqrt(mean_square + epsilon) * gain_vec).astype(jnp.bfloat16)


def body(n_patch, timestep, length, tokens, mod, w_qkv, q_gain, k_gain, w_out, stale, update, new_kv,
         tok_v, mod_v, w_v, wo_v, rows_v, q_v, kv_v, far, num, den, att, att_in,
         local_sem, head_sem, send_sem, recv_sem):
    tok_dev = tokens.shape[0]
    patch_rows = 2 * tok_dev
    half_rows = patch_rows // 2
    width = w_qkv.shape[2]
    heads = width // HD
    text_rows = 4 * patch_rows
    n_z = n_patch // 2
    inverse_root = 1.0 / math.sqrt(HD)

    me = lax.axis_index("patch")
    core = lax.axis_index("head")
    z, x = lax.div(me, 2), lax.rem(me, 2)
    xp = 1 - x
    has_up, has_down = z < n_z - 1, z > 0
    targets = {ACROSS: 2 * z + xp, DOWN: me - 2, UP: me + 2}

    def local(src, dst, at):
        return pltpu.make_async_copy(src, dst, local_sem.at[at])

    loads = [local(tokens, tok_v, 0), local(mod, mod_v, 1)]
    loads += [local(w_qkv.at[i], w_v.at[i], 2 + i) for i in range(3)]
    loads += [local(w_out, wo_v, 5)]
    for load in loads:
        load.start()

    barrier = pltpu.get_barrier_semaphore()
    pl.semaphore_signal(barrier, inc=1, device_id={"head": 1 - core}, device_id_type=MESH)
    pl.semaphore_signal(barrier, inc=1, device_id={"patch": targets[ACROSS]}, device_id_type=MESH)

    @pl.when(has_up)
    def _():
        pl.semaphore_signal(barrier, inc=1, device_id={"patch": targets[UP]}, device_id_type=MESH)

    @pl.when(has_down)
    def _():
        pl.semaphore_signal(barrier, inc=1, device_id={"patch": targets[DOWN]}, device_id_type=MESH)

    pl.semaphore_wait(barrier, 2 + has_up.astype(jnp.int32) + has_down.astype(jnp.int32))

    def piece(p, half):
        return far.at[p, :, pl.ds(half * half_rows, half_rows), :]

    def send(p, half, way, own=False):
        src = stale.at[:, pl.ds(half * half_rows, half_rows), :] if own else piece(p, half)
        return pltpu.make_async_remote_copy(
            src_ref=src, dst_ref=piece(p, half),
            send_sem=send_sem.at[way, p, half], recv_sem=recv_sem.at[p, half],
            device_id={"patch": targets[way]}, device_id_type=MESH,
        )

    def own_sends(act):
        for half, zhalf in ((1, 0), (0, 1)):
            act(send(me, half, ACROSS, True))

            @pl.when(has_up)
            def _():
                act(send(me, zhalf, UP, True))

            @pl.when(has_down)
            def _():
                act(send(me, zhalf, DOWN, True))

    def forward(d, half, act):
        up, down = z + d, z - d

        @pl.when(up < n_z)
        def _():
            p = 2 * up + x
            if act is start:
                send(p, half, ACROSS).wait_recv()

            @pl.when(has_down)
            def _():
                act(send(p, half, DOWN))

            @pl.when((d > 1) | (half == 0))
            def _():
                act(send(p, half, ACROSS))

        @pl.when(down >= 0)
        def _():
            p = 2 * down + x
            if act is start:
                send(p, half, ACROSS).wait_recv()

            @pl.when(has_up)
            def _():
                act(send(p, half, UP))

            @pl.when((d > 1) | (half == 0))
            def _():
                act(send(p, half, ACROSS))

    def start(copy):
        copy.start()

    def drain(copy):
        copy.wait_send()

    own_sends(start)

    t = timestep[0]
    loads[0].wait()
    loads[1].wait()
    shift_row = mod_v[0, pl.ds(t, 1), :]
    scale_row = mod_v[1, pl.ds(t, 1), :]
    widened = tok_v[...].astype(jnp.float32)
    centred = widened - jnp.mean(widened, axis=-1, keepdims=True)
    variance = jnp.mean(centred * centred, axis=-1, keepdims=True)
    normed = centred * lax.rsqrt(variance + epsilon) * (1.0 + scale_row) + shift_row
    rows_v[core] = normed.astype(jnp.bfloat16)
    swap = pltpu.make_async_remote_copy(
        src_ref=rows_v.at[core], dst_ref=rows_v.at[core],
        send_sem=head_sem.at[0], recv_sem=head_sem.at[1],
        device_id={"head": 1 - core}, device_id_type=MESH,
    )
    swap.start()
    swap.wait_recv()

    rows = rows_v[...].reshape(patch_rows, rows_v.shape[2])
    for part in range(3):
        loads[2 + part].wait()
        mixed = jnp.dot(rows, w_v[part], preferred_element_type=jnp.float32)
        if part == 2:
            kv_v[1] = mixed.astype(jnp.bfloat16)
            continue
        gain = (q_gain if part == 0 else k_gain)[...]
        for h in range(heads):
            cols = slice(h * HD, (h + 1) * HD)
            scaled = rms_scaled(mixed[:, cols], gain)
            if part == 0:
                q_v[:, cols] = scaled
            else:
                kv_v[0, :, cols] = scaled
    store_kv = local(kv_v, new_kv, 6)
    store_kv.start()

    limit = length[0]
    lane = lax.broadcasted_iota(jnp.int32, (1, patch_rows), 1)

    def attend(keys, p, first):
        position = p * patch_rows + lane
        visible = ((position >= text_rows) | (position < limit)).astype(jnp.float32)
        for h in range(heads):
            cols = slice(h * HD, (h + 1) * HD)
            scores = lax.dot_general(
                q_v[:, cols], keys[0, :, cols], (((1,), (1,)), ((), ())),
                preferred_element_type=jnp.float32,
            ) * inverse_root
            exps = jnp.exp(scores) * visible
            part = jnp.dot(exps.astype(jnp.bfloat16), keys[1, :, cols],
                           preferred_element_type=jnp.float32)
            if first:
                den[h] = exps
                num[:, cols] = part
            else:
                den[h] += exps
                num[:, cols] += part

    def attend_far(p):
        attend(far.at[p], p, False)

    def attend_across(up_ok, p):
        @pl.when(up_ok)
        def _():
            send(p, 0, ACROSS).wait_recv()
            send(p, 1, ACROSS).wait_recv()
            attend_far(p)

    attend(kv_v, me, True)

    peer = 2 * z + xp
    send(peer, 1, ACROSS).wait_recv()

    @pl.when(z == n_z - 1)
    def _():
        send(peer, 1, DOWN).start()

    @pl.when(z == 0)
    def _():
        send(peer, 1, UP).start()

    def step(d, carry):
        up, down = z + d, z - d
        forward(d, 0, start)
        forward(d, 1, start)

        @pl.when((up == n_z - 1) & has_down)
        def _():
            send(peer, 1, DOWN).start()

        @pl.when((down == 0) & has_up)
        def _():
            send(peer, 1, UP).start()

        @pl.when(up < n_z)
        def _():
            attend_far(2 * up + x)

        @pl.when(down >= 0)
        def _():
            attend_far(2 * down + x)

        @pl.when(d == 1)
        def _():
            send(peer, 0, ACROSS).wait_recv()
            attend_far(peer)

        attend_across((d > 2) & (up - 1 < n_z), 2 * (up - 1) + xp)
        attend_across((d > 2) & (down + 1 >= 0), 2 * (down + 1) + xp)
        return carry

    lax.fori_loop(1, n_z, step, 0)
    if n_z > 2:
        attend_across(z == 0, 2 * (n_z - 1) + xp)
        attend_across(z == n_z - 1, xp)
    attend_across(has_up, 2 * (z + 1) + xp)
    attend_across(has_down, 2 * (z - 1) + xp)

    for h in range(heads):
        cols = slice(h * HD, (h + 1) * HD)
        total = jnp.sum(den[h], axis=-1, keepdims=True)
        merged = (num[:, cols] / total).astype(jnp.bfloat16)
        att[:, :, cols] = merged.reshape(2, tok_dev, HD)
    back = pltpu.make_async_remote_copy(
        src_ref=att.at[1 - core], dst_ref=att_in,
        send_sem=head_sem.at[2], recv_sem=head_sem.at[3],
        device_id={"head": 1 - core}, device_id_type=MESH,
    )
    back.start()
    loads[5].wait()
    mine = pl.ds(pl.multiple_of(core * width, width), width)
    theirs = pl.ds(pl.multiple_of((1 - core) * width, width), width)
    projected = jnp.dot(att[core], wo_v[mine, :], preferred_element_type=jnp.float32)
    back.wait_recv()
    projected += jnp.dot(att_in[...], wo_v[theirs, :], preferred_element_type=jnp.float32)
    update[...] = (mod_v[2, pl.ds(t, 1), :] * projected).astype(jnp.bfloat16)

    swap.wait_send()
    back.wait_send()
    store_kv.wait()
    own_sends(drain)

    @pl.when(has_up)
    def _():
        send(peer, 1, UP).wait_send()

    @pl.when(has_down)
    def _():
        send(peer, 1, DOWN).wait_send()

    def drain_step(d, carry):
        forward(d, 0, drain)
        forward(d, 1, drain)
        return carry

    lax.fori_loop(1, n_z, drain_step, 0)


def shards(n_patch, tokens, timestep, text_length, mod_table, w_qkv, q_gain, k_gain, w_out, stale_kv):
    tok_dev, model = tokens.shape
    rows = 2 * tok_dev
    width = w_qkv.shape[2]
    heads = width // HD
    bf, f32 = jnp.bfloat16, jnp.float32
    vmem, smem, anywhere = (pl.BlockSpec(memory_space=m) for m in (pltpu.VMEM, pltpu.SMEM, pl.ANY))
    mod = jnp.transpose(mod_table, (1, 0, 2))
    w = jnp.transpose(w_qkv, (1, 0, 2))

    def kernel(*refs):
        body(n_patch, *refs)

    return pl.pallas_call(
        kernel,
        out_shape=(
            jax.ShapeDtypeStruct((tok_dev, model), bf),
            jax.ShapeDtypeStruct((2, rows, width), bf),
        ),
        in_specs=[smem, smem, anywhere, anywhere, anywhere, vmem, vmem, anywhere, anywhere],
        out_specs=(vmem, anywhere),
        scratch_shapes=[
            pltpu.VMEM((tok_dev, model), bf),
            pltpu.VMEM(mod.shape, f32),
            pltpu.VMEM(w.shape, bf),
            pltpu.VMEM(w_out.shape, bf),
            pltpu.VMEM((2, tok_dev, model), bf),
            pltpu.VMEM((rows, width), bf),
            pltpu.VMEM((2, rows, width), bf),
            pltpu.VMEM((n_patch, 2, rows, width), bf),
            pltpu.VMEM((rows, width), f32),
            pltpu.VMEM((heads, rows, rows), f32),
            pltpu.VMEM((2, tok_dev, width), bf),
            pltpu.VMEM((tok_dev, width), bf),
            pltpu.SemaphoreType.DMA((7,)),
            pltpu.SemaphoreType.DMA((4,)),
            pltpu.SemaphoreType.DMA((3, n_patch, 2)),
            pltpu.SemaphoreType.DMA((n_patch, 2)),
        ],
        compiler_params=pltpu.CompilerParams(
            collective_id=0, has_side_effects=True, vmem_limit_bytes=52 * 1024 * 1024
        ),
    )(timestep, text_length, tokens, mod, w, q_gain.reshape(1, HD), k_gain.reshape(1, HD), w_out, stale_kv)


def solution(mesh):
    n_patch = mesh.shape["patch"]

    def local(*args):
        return shards(n_patch, *args)

    return jax.shard_map(
        local,
        mesh=mesh,
        in_specs=(
            P(("groups", "patch", "head"), None),
            P("groups"),
            P("groups"),
            P(),
            P(None, None, "head"),
            P(),
            P(),
            P(),
            P(None, ("groups", "patch"), "head"),
        ),
        out_specs=(P(("groups", "patch", "head"), None), P(None, ("groups", "patch"), "head")),
        check_vma=False,
    )
```

time: 98 us -> 49.8 us (0.51)
  waiting for transfers between devices: 51.6 us -> 0 us
  Pallas kernels: 0 us -> 41.2 us
  between operations: 15.6 us -> 1.94 us
  local copies, waits for them, and re-layouts: 15.2 us -> 5.71 us
  matrix products: 8.9 us -> 0 us
  other arithmetic: 4.06 us -> 0 us
  blocking collectives: 2.16 us -> 0 us
    all_gather x1 -> x0, waiting for transfers between devices: 46.4 us -> none  [shards(): gathered = lax.all_gather(stale_kv, 'patch', axis=1, tiled=True)]
    pallas_call x0 -> x1, Pallas kernels: none -> 41.2 us  [shards(): pl.pallas_call(kernel, out_shape=(jax.ShapeDtypeStruct((tok_dev, model),...]
    dot_general x6 -> x0, matrix products: 8.9 us -> none  [the longest x1 5.01 us: shards(): jnp.dot(lax.all_gather(normed, 'head', axis=0, tiled=True), w_local, pref...]
    unnamed x12, local copies, waits for them, and re-layouts: 12.3 us -> 5.71 us
    reduce_scatter x1 -> x0, waiting for transfers between devices: 5.16 us -> none  [shards(): lax.psum_scatter(jnp.dot(attention, w_rows, preferred_element_type=jnp.fl...]
    slice x3 -> x0, local copies, waits for them, and re-layouts: 2.4 us -> none  [the longest x1 2.35 us: shards(): gathered[0].reshape(all_rows, heads_dev, HD)]
    all_gather x1 -> x0, blocking collectives: 2.16 us -> none  [shards(): lax.all_gather(normed, 'head', axis=0, tiled=True)]
    convert_element_type x5 -> x0, other arithmetic: 1.91 us -> none  [the longest x1 1.7 us: shards(): update = (gate_row * projected).astype(jnp.bfloat16)]
  transfers between devices with their start and end apart: 2 -> 0, of which waited for: 2 -> 0; matrix products, arithmetic and copies ran while one was open for 19% -> 0% of each run, Pallas kernels for 0% -> 0%
where the time goes in v1:
time: 49.8 us; the launch traced here: 48.8 us
  Pallas kernels  41.2 us (83%)
  local copies, waits for them, and re-layouts  5.71 us (11%)
  between operations  1.94 us (4%)
    pallas_call x1, Pallas kernels, shards(): pl.pallas_call(kernel, out_shape=(jax.ShapeDtypeStruct((tok_dev, model),...  41.2 us
    unnamed x12, local copies, waits for them, and re-layouts  5.71 us

profile of v1, /device:TPU:0, one launch (start us, length us, event | category | flops | bytes accessed | tf_op | source)
XLA Modules:
  0.0 48.8 jit_solution(16303349948556167319)
XLA Ops:
  1.9 0.0 copy-start
  1.9 1.1 %copy-done = f32[28,3,1536]{2,0,1:T(8,128)S(1)} copy-done((f32[28,3,1536]{2,0,1:T(8,128)S(1)}, f32[28,3,1536]{2,0,1:T(8,128)}, u32[]{:S(2)}) %copy-start) | copy-done | bytes 516120
  3.0 0.0 copy-start.1
  3.0 1.0 %copy-done.1 = bf16[2,128,768]{2,1,0:T(8,128)(2,1)S(1)} copy-done((bf16[2,128,768]{2,1,0:T(8,128)(2,1)S(1)}, bf16[2,128,768]{2,1,0:T(8,128)(2,1)}, u32[]{:S(2)}) %copy-start.1) | copy-done | bytes 393240
  4.0 0.0 copy-start.2
  4.0 0.9 %copy-done.2 = bf16[64,1536]{1,0:T(8,128)(2,1)S(1)} copy-done((bf16[64,1536]{1,0:T(8,128)(2,1)S(1)}, bf16[64,1536]{1,0:T(8,128)(2,1)}, u32[]{:S(2)}) %copy-start.2) | copy-done | bytes 196632
  4.9 0.0 copy-start.3
  4.9 0.7 %copy-done.3 = f32[128]{0:T(128)S(1)} copy-done((f32[128]{0:T(128)S(1)}, f32[128]{0:T(128)}, u32[]{:S(2)}) %copy-start.3) | copy-done | bytes 536
  5.6 0.0 copy-start.4
  5.6 0.7 %copy-done.4 = f32[128]{0:T(128)S(1)} copy-done((f32[128]{0:T(128)S(1)}, f32[128]{0:T(128)}, u32[]{:S(2)}) %copy-start.4) | copy-done | bytes 536
  6.2 41.2 %shard_map.104 = (bf16[64,1536]{1,0:T(8,128)(2,1)S(1)}, bf16[2,128,768]{2,1,0:T(8,128)(2,1)S(1)}) custom-call(s32[1]{0:T(128)S(6)} %copy.13.refs_0_, s32[1]{0:T(128)S(6)} %copy.14.refs_1_, bf16[64,1536]{1,0:T(8,128)(2,1)S(1)} %copy-done.2, f32[3,28,1536]{2,1,0:T(8,128)S(1)} %bitcast.4, bf16[3,1536,768]{2,1,0:T(8,128)(2,1)} %bitcast.7, f32[1,128]{1,0:T(1,128)S(1)} %bitcast.5, ...), custom_call_target="tpu_custom_call" | custom-call | tf_op jit(solution)/shard_map/pallas_call | solution.py:296
  47.4 0.7 %copy.15 = bf16[64,1536]{1,0:T(8,128)(2,1)} copy(bf16[64,1536]{1,0:T(8,128)(2,1)S(1)} %get-tuple-element.4) | data formatting | bytes 393216
  48.1 0.7 %copy.16 = bf16[2,128,768]{2,1,0:T(8,128)(2,1)} copy(bf16[2,128,768]{2,1,0:T(8,128)(2,1)S(1)} %get-tuple-element.5) | data formatting | bytes 786432
Async XLA Ops:
  1.9 1.1 %copy-start = (f32[28,3,1536]{2,0,1:T(8,128)S(1)}, f32[28,3,1536]{2,0,1:T(8,128)}, u32[]{:S(2)}) copy-start(f32[28,3,1536]{2,0,1:T(8,128)} %param.12) | copy-start | bytes 1548292
  3.0 1.0 %copy-start.1 = (bf16[2,128,768]{2,1,0:T(8,128)(2,1)S(1)}, bf16[2,128,768]{2,1,0:T(8,128)(2,1)}, u32[]{:S(2)}) copy-start(bf16[2,128,768]{2,1,0:T(8,128)(2,1)} %refs_8_.1) | copy-start | bytes 1179652
  4.0 0.9 %copy-start.2 = (bf16[64,1536]{1,0:T(8,128)(2,1)S(1)}, bf16[64,1536]{1,0:T(8,128)(2,1)}, u32[]{:S(2)}) copy-start(bf16[64,1536]{1,0:T(8,128)(2,1)} %refs_2_.1) | copy-start | bytes 589828
  4.9 0.7 %copy-start.3 = (f32[128]{0:T(128)S(1)}, f32[128]{0:T(128)}, u32[]{:S(2)}) copy-start(f32[128]{0:T(128)} %param.14) | copy-start | bytes 1540
  5.6 0.7 %copy-start.4 = (f32[128]{0:T(128)S(1)}, f32[128]{0:T(128)}, u32[]{:S(2)}) copy-start(f32[128]{0:T(128)} %param.15) | copy-start | bytes 1540

commit v2 on v1

v2 whole, which is shorter than its diff:
```python
import math

import jax
import jax.numpy as jnp
from jax import lax
from jax.experimental import pallas as pl
from jax.experimental.pallas import tpu as pltpu
from jax.sharding import PartitionSpec as P

HD = 128
epsilon = 1e-06
MESH = pl.DeviceIdType.MESH
ACROSS, DOWN, UP = 0, 1, 2


def rms_scaled(values, gain_vec):
    mean_square = jnp.mean(values * values, axis=-1, keepdims=True)
    return (values * lax.rsqrt(mean_square + epsilon) * gain_vec).astype(jnp.bfloat16)


def body(n_patch, timestep, length, tokens, mod, w_qkv, q_gain, k_gain, w_out, stale, update, new_kv,
         tok_v, mod_v, gain_v, w_v, wo_v, rows_v, fresh, kv_v, far, group, num, den, out_v, att,
         local_sem, head_sem, kv_send, kv_recv, fresh_send, fresh_recv, out_send, out_recv):
    tok_dev = tokens.shape[0]
    patch_rows = 2 * tok_dev
    width = w_qkv.shape[2]
    heads = width // HD
    per_col = heads // 2
    text_rows = 4 * patch_rows
    n_z = n_patch // 2
    inverse_root = 1.0 / math.sqrt(HD)

    me = lax.axis_index("patch")
    core = lax.axis_index("head")
    z, x = lax.div(me, 2), lax.rem(me, 2)
    xp = 1 - x
    level = lax.rem(z, 2)
    base = me - 2 * level - x
    slot = 2 * level + x
    peer = 2 * z + xp
    targets = {ACROSS: peer, DOWN: me - 2, UP: me + 2}

    def side(j, at_core):
        return (0, at_core, 1)[j]

    def goes_up(j):
        return (z < n_z - 1) & ((z < n_z - 2) | (side(j, core) == 1))

    def goes_down(j):
        return (z > 0) & ((z > 1) | (side(j, core) == 0))

    def owned(j):
        return level == side(j, core)

    def local(src, dst, at):
        return pltpu.make_async_copy(src, dst, local_sem.at[at])

    def head_cols(l):
        return pl.ds(pl.multiple_of(l * HD, HD), HD)

    loads = [local(tokens, tok_v, 0), local(mod, mod_v, 1)]
    loads += [local(w_qkv.at[i], w_v.at[i], 2 + i) for i in range(3)]
    loads += [local(w_out, wo_v, 5)]
    loads += [local(q_gain, gain_v.at[0], 7), local(k_gain, gain_v.at[1], 8)]
    loads += [local(stale.at[:, :, head_cols(3 * x + j)], far.at[me, j], 9 + j) for j in range(3)]
    for i in (0, 1, 6, 7, 2, 3, 4, 8, 9, 10, 5):
        loads[i].start()

    barrier = pltpu.get_barrier_semaphore()
    for s in range(4):
        for cc in range(2):
            @pl.when((slot != s) | (core != cc))
            def _(s=s, cc=cc):
                pl.semaphore_signal(barrier, inc=1, device_id={"patch": base + s, "head": cc},
                                    device_id_type=MESH)

    out_up = (level == 1) & (z < n_z - 1)
    out_down = (level == 0) & (z > 0)

    @pl.when(out_up)
    def _():
        pl.semaphore_signal(barrier, inc=1, device_id={"patch": me + 2}, device_id_type=MESH)

    @pl.when(out_down)
    def _():
        pl.semaphore_signal(barrier, inc=1, device_id={"patch": me - 2}, device_id_type=MESH)

    num[...] = jnp.zeros_like(num)
    den[...] = jnp.zeros_like(den)
    pl.semaphore_wait(barrier, 7 + out_up.astype(jnp.int32) + out_down.astype(jnp.int32))

    def send(p, j, way, src=None):
        return pltpu.make_async_remote_copy(
            src_ref=far.at[p, j] if src is None else src, dst_ref=far.at[p, j],
            send_sem=kv_send.at[way, p, j], recv_sem=kv_recv.at[p, j],
            device_id={"patch": targets[way]}, device_id_type=MESH,
        )

    def start(copy):
        copy.start()

    def drain(copy):
        copy.wait_send()

    def own_sends(act):
        for j in (0, 2, 1):
            act(send(me, j, ACROSS, stale.at[:, :, head_cols(3 * xp + j)]))
        for i in range(3):
            @pl.when(goes_up(2 - i))
            def _(j=2 - i):
                act(send(me, j, UP, stale.at[:, :, head_cols(3 * x + j)]))

            @pl.when(goes_down(i))
            def _(j=i):
                act(send(me, j, DOWN, stale.at[:, :, head_cols(3 * x + j)]))

    def peer_sends(act):
        for i in range(3):
            @pl.when(goes_up(2 - i))
            def _(j=2 - i):
                act(send(peer, j, UP))

            @pl.when(goes_down(i))
            def _(j=i):
                act(send(peer, j, DOWN))

    def forward(d, col, act):
        up, down = z + d, z - d
        for i in range(3):
            @pl.when((up < n_z) & ((z > 0) | (side(i, core) == 0)))
            def _(j=i):
                p = 2 * up + col
                if act is start:
                    send(p, j, ACROSS).wait_recv()

                @pl.when(goes_down(j))
                def _():
                    act(send(p, j, DOWN))

            @pl.when((down >= 0) & ((z < n_z - 1) | (side(2 - i, core) == 1)))
            def _(j=2 - i):
                p = 2 * down + col
                if act is start:
                    send(p, j, ACROSS).wait_recv()

                @pl.when(goes_up(j))
                def _():
                    act(send(p, j, UP))

    own_sends(start)

    t = timestep[0]
    loads[0].wait()
    loads[1].wait()
    shift_row = mod_v[0, pl.ds(t, 1), :]
    scale_row = mod_v[1, pl.ds(t, 1), :]
    widened = tok_v[...].astype(jnp.float32)
    centred = widened - jnp.mean(widened, axis=-1, keepdims=True)
    variance = jnp.mean(centred * centred, axis=-1, keepdims=True)
    normed = centred * lax.rsqrt(variance + epsilon) * (1.0 + scale_row) + shift_row
    rows_v[core] = normed.astype(jnp.bfloat16)
    swap = pltpu.make_async_remote_copy(
        src_ref=rows_v.at[core], dst_ref=rows_v.at[core],
        send_sem=head_sem.at[0], recv_sem=head_sem.at[1],
        device_id={"head": 1 - core}, device_id_type=MESH,
    )
    swap.start()
    swap.wait_recv()
    loads[6].wait()
    loads[7].wait()

    rows = rows_v[...].reshape(patch_rows, rows_v.shape[2])
    for part in range(3):
        loads[2 + part].wait()
        mixed = jnp.dot(rows, w_v[part], preferred_element_type=jnp.float32)
        for h in range(heads):
            cols = slice(h * HD, (h + 1) * HD)
            if part == 2:
                value = mixed[:, cols].astype(jnp.bfloat16)
            else:
                value = rms_scaled(mixed[:, cols], gain_v[part])
            fresh[h, part] = value
            if part > 0:
                kv_v[part - 1, :, cols] = value

    def fresh_copy(l):
        j = l % 3
        owner = base + 2 * side(j, core) + l // 3
        return pltpu.make_async_remote_copy(
            src_ref=fresh.at[l], dst_ref=group.at[j, slot],
            send_sem=fresh_send.at[l], recv_sem=fresh_recv.at[j, slot],
            device_id={"patch": owner}, device_id_type=MESH,
        )

    def fresh_here(l):
        return owned(l % 3) & (x == l // 3)

    def fresh_sends(act):
        for l in range(heads):
            @pl.when(jnp.logical_not(fresh_here(l)))
            def _(l=l):
                act(fresh_copy(l))

    fresh_sends(start)
    for l in range(heads):
        @pl.when(fresh_here(l))
        def _(l=l):
            group[l % 3, slot] = fresh[l]
    store_kv = local(kv_v, new_kv, 6)
    store_kv.start()

    for i in (0, 2, 1):
        send(peer, i, ACROSS).wait_recv()
    peer_sends(start)

    limit = length[0]
    lane = lax.broadcasted_iota(jnp.int32, (1, patch_rows), 1)
    all_rows = 4 * patch_rows
    row_slot = lax.div(lax.broadcasted_iota(jnp.int32, (all_rows, 1), 0), patch_rows)

    def seen(p):
        position = p * patch_rows + lane
        return (position >= text_rows) | (position < limit)

    def contract(queries, keys):
        return lax.dot_general(queries, keys, (((1,), (1,)), ((), ())),
                               preferred_element_type=jnp.float32) * inverse_root

    def attend(p):
        mask = seen(p) & (row_slot != p - base)

        def head(j):
            queries = group[j, :, 0].reshape(all_rows, HD)
            exps = jnp.where(mask, jnp.exp(contract(queries, far[p, j, 0])), 0.0)
            den[j] += exps
            num[j] += jnp.dot(exps.astype(jnp.bfloat16), far[p, j, 1],
                              preferred_element_type=jnp.float32)

        head(2 * level)

        @pl.when(owned(1))
        def _():
            head(1)

    def attend_fresh(j):
        for s in range(4):
            own = slice(s * patch_rows, (s + 1) * patch_rows)
            exps = jnp.where(seen(base + s), jnp.exp(contract(group[j, s, 0], group[j, s, 1])), 0.0)
            den[j, own] += exps
            num[j, own] += jnp.dot(exps.astype(jnp.bfloat16), group[j, s, 2],
                                   preferred_element_type=jnp.float32)

    def attend_level(d, col):
        @pl.when(z + d < n_z)
        def _():
            attend(2 * (z + d) + col)

        @pl.when(z - d >= 0)
        def _():
            attend(2 * (z - d) + col)

    forward(1, x, start)
    forward(1, xp, start)

    for j in range(3):
        loads[8 + j].wait()

        @pl.when(owned(j))
        def _(j=j):
            for s in range(4):
                @pl.when(slot != s)
                def _(s=s):
                    pltpu.make_async_remote_copy(
                        src_ref=group.at[j, s], dst_ref=group.at[j, s],
                        send_sem=fresh_send.at[j], recv_sem=fresh_recv.at[j, s],
                        device_id={"patch": peer}, device_id_type=MESH,
                    ).wait_recv()
            attend_fresh(j)

    attend(me)
    attend(peer)
    attend_level(1, x)

    def step(d, carry):
        forward(d, x, start)
        attend_level(d - 1, xp)
        forward(d, xp, start)
        attend_level(d, x)
        return carry

    lax.fori_loop(2, n_z, step, 0)
    attend_level(n_z - 1, xp)

    def out_copy(j, s, cc):
        return pltpu.make_async_remote_copy(
            src_ref=out_v.at[j, s, cc], dst_ref=att.at[:, head_cols(heads * core + 3 * x + j)],
            send_sem=out_send.at[j, s, cc], recv_sem=out_recv.at[heads * core + 3 * x + j],
            device_id={"patch": base + s, "head": cc}, device_id_type=MESH,
        )

    def out_sends(j, act):
        for s in range(4):
            for cc in range(2):
                @pl.when((slot != s) | (core != cc))
                def _(s=s, cc=cc):
                    act(out_copy(j, s, cc))

    for j in range(3):
        @pl.when(owned(j))
        def _(j=j):
            total = jnp.sum(den[j], axis=-1, keepdims=True)
            merged = (num[j] / total).astype(jnp.bfloat16)
            out_v[j] = merged.reshape(4, 2, tok_dev, HD)
            out_sends(j, start)
            att[:, head_cols(heads * core + 3 * x + j)] = out_v[j, slot, core]

    loads[5].wait()
    for g in range(2 * heads):
        l = g % heads
        at_core, col, j = g // heads, l // 3, l % 3
        here = (core == at_core) & (x == col) & (level == side(j, at_core))

        @pl.when(jnp.logical_not(here))
        def _(g=g):
            pltpu.make_async_remote_copy(
                src_ref=out_v.at[0, 0, 0], dst_ref=att.at[:, pl.ds(g * HD, HD)],
                send_sem=out_send.at[0, 0, 0], recv_sem=out_recv.at[g],
                device_id={"patch": peer}, device_id_type=MESH,
            ).wait_recv()

    projected = jnp.dot(att[...], wo_v[...], preferred_element_type=jnp.float32)
    update[...] = (mod_v[2, pl.ds(t, 1), :] * projected).astype(jnp.bfloat16)

    swap.wait_send()
    store_kv.wait()
    own_sends(drain)
    peer_sends(drain)
    fresh_sends(drain)
    for j in range(3):
        @pl.when(owned(j))
        def _(j=j):
            out_sends(j, drain)

    def drain_step(d, carry):
        forward(d, x, drain)
        forward(d, xp, drain)
        return carry

    lax.fori_loop(1, n_z, drain_step, 0)


def shards(n_patch, tokens, timestep, text_length, mod_table, w_qkv, q_gain, k_gain, w_out, stale_kv):
    tok_dev, model = tokens.shape
    rows = 2 * tok_dev
    width = w_qkv.shape[2]
    heads = width // HD
    bf, f32 = jnp.bfloat16, jnp.float32
    vmem, smem, anywhere = (pl.BlockSpec(memory_space=m) for m in (pltpu.VMEM, pltpu.SMEM, pl.ANY))
    mod = jnp.transpose(mod_table, (1, 0, 2))
    w = jnp.transpose(w_qkv, (1, 0, 2))

    def kernel(*refs):
        body(n_patch, *refs)

    dma = pltpu.SemaphoreType.DMA
    return pl.pallas_call(
        kernel,
        out_shape=(
            jax.ShapeDtypeStruct((tok_dev, model), bf),
            jax.ShapeDtypeStruct((2, rows, width), bf),
        ),
        in_specs=[smem, smem] + [anywhere] * 7,
        out_specs=(vmem, anywhere),
        scratch_shapes=[
            pltpu.VMEM((tok_dev, model), bf),
            pltpu.VMEM(mod.shape, f32),
            pltpu.VMEM((2, 1, HD), f32),
            pltpu.VMEM(w.shape, bf),
            pltpu.VMEM(w_out.shape, bf),
            pltpu.VMEM((2, tok_dev, model), bf),
            pltpu.VMEM((heads, 3, rows, HD), bf),
            pltpu.VMEM((2, rows, width), bf),
            pltpu.VMEM((n_patch, 3, 2, rows, HD), bf),
            pltpu.VMEM((3, 4, 3, rows, HD), bf),
            pltpu.VMEM((3, 4 * rows, HD), f32),
            pltpu.VMEM((3, 4 * rows, HD), f32),
            pltpu.VMEM((3, 4, 2, tok_dev, HD), bf),
            pltpu.VMEM((tok_dev, model), bf),
            dma((12,)),
            dma((2,)),
            dma((3, n_patch, 3)),
            dma((n_patch, 3)),
            dma((heads,)),
            dma((3, 4)),
            dma((3, 4, 2)),
            dma((2 * heads,)),
        ],
        compiler_params=pltpu.CompilerParams(
            collective_id=0, has_side_effects=True, vmem_limit_bytes=63 * 1024 * 1024
        ),
    )(timestep, text_length, tokens, mod, w, q_gain.reshape(1, HD), k_gain.reshape(1, HD), w_out, stale_kv)


def solution(mesh):
    n_patch = mesh.shape["patch"]

    def local(*args):
        return shards(n_patch, *args)

    return jax.shard_map(
        local,
        mesh=mesh,
        in_specs=(
            P(("groups", "patch", "head"), None),
            P("groups"),
            P("groups"),
            P(),
            P(None, None, "head"),
            P(),
            P(),
            P(),
            P(None, ("groups", "patch"), "head"),
        ),
        out_specs=(P(("groups", "patch", "head"), None), P(None, ("groups", "patch"), "head")),
        check_vma=False,
    )
```

time: 49.8 us -> 43.1 us (0.87); the launches traced: 48.8 us -> 42.9 us
  Pallas kernels: 41.2 us -> 37.5 us
  local copies, waits for them, and re-layouts: 5.71 us -> 3.38 us
    pallas_call x1, Pallas kernels: 41.2 us -> 37.5 us  [shards(): pl.pallas_call(kernel, out_shape=(jax.ShapeDtypeStruct((tok_dev, model),...]
    unnamed x12 -> x2, local copies, waits for them, and re-layouts: 5.71 us -> 3.38 us
where the time goes in v2:
time: 43.1 us; the launch traced here: 42.9 us
  Pallas kernels  37.5 us (87%)
  local copies, waits for them, and re-layouts  3.38 us (8%)
  between operations  1.93 us (4%)
    pallas_call x1, Pallas kernels, shards(): pl.pallas_call(kernel, out_shape=(jax.ShapeDtypeStruct((tok_dev, model),...  37.5 us
    unnamed x2, local copies, waits for them, and re-layouts  3.38 us

profile of v2, /device:TPU:0, one launch (start us, length us, event | category | flops | bytes accessed | tf_op | source)
XLA Modules:
  0.0 42.9 jit_solution(10619404764045507404)
XLA Ops:
  1.9 37.5 %shard_map.104 = (bf16[64,1536]{1,0:T(8,128)(2,1)}, bf16[2,128,768]{2,1,0:T(8,128)(2,1)}) custom-call(s32[1]{0:T(128)S(6)} %copy.13.refs_0_, s32[1]{0:T(128)S(6)} %copy.14.refs_1_, bf16[64,1536]{1,0:T(8,128)(2,1)} %refs_2_.1, f32[3,28,1536]{2,1,0:T(8,128)} %bitcast.5, bf16[3,1536,768]{2,1,0:T(8,128)(2,1)} %bitcast.4, f32[1,128]{1,0:T(1,128)} %bitcast.6, ...), custom_call_target="tpu_custom_call" | custom-call | tf_op jit(solution)/shard_map/pallas_call | solution.py:366
  39.5 1.6 %copy.15 = bf16[64,1536]{1,0:T(8,128)(2,1)} copy(bf16[64,1536]{1,0:T(8,128)(2,1)} %get-tuple-element.4) | data formatting | bytes 393216
  41.1 1.8 %copy.16 = bf16[2,128,768]{2,1,0:T(8,128)(2,1)} copy(bf16[2,128,768]{2,1,0:T(8,128)(2,1)} %get-tuple-element.5) | data formatting | bytes 786432

commit v3 on v2

--- a/solution.py
+++ b/solution.py
@@ -261,6 +261,8 @@
 
     forward(1, x, start)
     forward(1, xp, start)
+    if n_z > 2:
+        forward(2, x, start)
 
     for j in range(3):
         loads[8 + j].wait()
@@ -281,6 +283,11 @@
     attend(peer)
     attend_level(1, x)
 
+    if n_z > 2:
+        forward(2, xp, start)
+        attend_level(1, xp)
+        attend_level(2, x)
+
     def step(d, carry):
         forward(d, x, start)
         attend_level(d - 1, xp)
@@ -288,7 +295,7 @@
         attend_level(d, x)
         return carry
 
-    lax.fori_loop(2, n_z, step, 0)
+    lax.fori_loop(3, n_z, step, 0)
     attend_level(n_z - 1, xp)
 
     def out_copy(j, s, cc):
@@ -314,6 +321,18 @@
             out_sends(j, start)
             att[:, head_cols(heads * core + 3 * x + j)] = out_v[j, slot, core]
 
+    swap.wait_send()
+    store_kv.wait()
+    own_sends(drain)
+    peer_sends(drain)
+    fresh_sends(drain)
+    def drain_step(d, carry):
+        forward(d, x, drain)
+        forward(d, xp, drain)
+        return carry
+
+    lax.fori_loop(1, n_z, drain_step, 0)
+
     loads[5].wait()
     for g in range(2 * heads):
         l = g % heads
@@ -331,22 +350,19 @@
     projected = jnp.dot(att[...], wo_v[...], preferred_element_type=jnp.float32)
     update[...] = (mod_v[2, pl.ds(t, 1), :] * projected).astype(jnp.bfloat16)
 
-    swap.wait_send()
-    store_kv.wait()
-    own_sends(drain)
-    peer_sends(drain)
-    fresh_sends(drain)
     for j in range(3):
         @pl.when(owned(j))
         def _(j=j):
             out_sends(j, drain)
 
-    def drain_step(d, carry):
-        forward(d, x, drain)
-        forward(d, xp, drain)
-        return carry
-
-    lax.fori_loop(1, n_z, drain_step, 0)
+
+def deliver(update, new_kv, update_out, new_kv_out, sem):
+    copies = [pltpu.make_async_copy(update, update_out, sem.at[0]),
+              pltpu.make_async_copy(new_kv, new_kv_out, sem.at[1])]
+    for copy in copies:
+        copy.start()
+    for copy in copies:
+        copy.wait()
 
 
 def shards(n_patch, tokens, timestep, text_length, mod_table, w_qkv, q_gain, k_gain, w_out, stale_kv):
@@ -363,7 +379,7 @@
         body(n_patch, *refs)
 
     dma = pltpu.SemaphoreType.DMA
-    return pl.pallas_call(
+    results = pl.pallas_call(
         kernel,
         out_shape=(
             jax.ShapeDtypeStruct((tok_dev, model), bf),
@@ -399,6 +415,13 @@
             collective_id=0, has_side_effects=True, vmem_limit_bytes=63 * 1024 * 1024
         ),
     )(timestep, text_length, tokens, mod, w, q_gain.reshape(1, HD), k_gain.reshape(1, HD), w_out, stale_kv)
+    return pl.pallas_call(
+        deliver,
+        out_shape=tuple(jax.ShapeDtypeStruct(r.shape, r.dtype) for r in results),
+        in_specs=[anywhere] * 2,
+        out_specs=(anywhere, anywhere),
+        scratch_shapes=[dma((2,))],
+    )(*results)
 
 
 def solution(mesh):

time: 43.1 us -> 58.1 us (1.35)
  Pallas kernels: 37.5 us -> 56 us
  local copies, waits for them, and re-layouts: 3.38 us -> 0 us
    pallas_call x0 -> x1, Pallas kernels: none -> 19 us  [shards(): pl.pallas_call(deliver, out_shape=tuple((jax.ShapeDtypeStruct(r.shape, r....]
    unnamed x2 -> x0, local copies, waits for them, and re-layouts: 3.38 us -> none
where the time goes in v3:
time: 58.1 us; the launch traced here: 57.9 us
  Pallas kernels  56 us (96%)
  between operations  1.93 us (3%)
    pallas_call x1, Pallas kernels, shards(): pl.pallas_call(kernel, out_shape=(jax.ShapeDtypeStruct((tok_dev, model),...  37 us
    pallas_call x1, Pallas kernels, shards(): pl.pallas_call(deliver, out_shape=tuple((jax.ShapeDtypeStruct(r.shape, r....  19 us

profile of v3, /device:TPU:0, one launch (start us, length us, event | category | flops | bytes accessed | tf_op | source)
XLA Modules:
  0.0 57.9 jit_solution(17698188545474449087)
XLA Ops:
  1.9 37.0 %shard_map.104 = (bf16[64,1536]{1,0:T(8,128)(2,1)}, bf16[2,128,768]{2,1,0:T(8,128)(2,1)}) custom-call(s32[1]{0:T(128)S(6)} %copy.11.refs_0_, s32[1]{0:T(128)S(6)} %copy.12.refs_1_, bf16[64,1536]{1,0:T(8,128)(2,1)} %refs_2_.1, f32[3,28,1536]{2,1,0:T(8,128)} %bitcast.5, bf16[3,1536,768]{2,1,0:T(8,128)(2,1)} %bitcast.4, f32[1,128]{1,0:T(1,128)} %bitcast.6, ...), custom_call_target="tpu_custom_call" | custom-call | tf_op jit(solution)/shard_map/pallas_call | solution.py:382
  38.9 19.0 %shard_map.105 = (bf16[64,1536]{1,0:T(8,128)(2,1)}, bf16[2,128,768]{2,1,0:T(8,128)(2,1)}) custom-call(bf16[64,1536]{1,0:T(8,128)(2,1)} %get-tuple-element.4.update, bf16[2,128,768]{2,1,0:T(8,128)(2,1)} %get-tuple-element.5.new_kv), custom_call_target="tpu_custom_call" | custom-call | tf_op jit(solution)/shard_map/pallas_call | solution.py:418

commit v4 on v3

--- a/solution.py
+++ b/solution.py
@@ -356,13 +356,18 @@
             out_sends(j, drain)
 
 
-def deliver(update, new_kv, update_out, new_kv_out, sem):
-    copies = [pltpu.make_async_copy(update, update_out, sem.at[0]),
-              pltpu.make_async_copy(new_kv, new_kv_out, sem.at[1])]
-    for copy in copies:
-        copy.start()
-    for copy in copies:
-        copy.wait()
+def deliver(update, new_kv, update_out, new_kv_out, update_v, kv_v, sem):
+    reads = [pltpu.make_async_copy(update, update_v, sem.at[0]),
+             pltpu.make_async_copy(new_kv, kv_v, sem.at[1])]
+    writes = [pltpu.make_async_copy(update_v, update_out, sem.at[2]),
+              pltpu.make_async_copy(kv_v, new_kv_out, sem.at[3])]
+    for read in reads:
+        read.start()
+    for read, write in zip(reads, writes):
+        read.wait()
+        write.start()
+    for write in writes:
+        write.wait()
 
 
 def shards(n_patch, tokens, timestep, text_length, mod_table, w_qkv, q_gain, k_gain, w_out, stale_kv):
@@ -420,7 +425,7 @@
         out_shape=tuple(jax.ShapeDtypeStruct(r.shape, r.dtype) for r in results),
         in_specs=[anywhere] * 2,
         out_specs=(anywhere, anywhere),
-        scratch_shapes=[dma((2,))],
+        scratch_shapes=[pltpu.VMEM(r.shape, r.dtype) for r in results] + [dma((4,))],
     )(*results)
 
 

time: 58.1 us -> 41 us (0.71)
  Pallas kernels: 56 us -> 38.9 us
    pallas_call x1, Pallas kernels: 19 us -> 1.88 us  [shards(): pl.pallas_call(deliver, out_shape=tuple((jax.ShapeDtypeStruct(r.shape, r....]
where the time goes in v4:
time: 41 us; the launch traced here: 40.8 us
  Pallas kernels  38.9 us (95%)
  between operations  1.93 us (5%)
    pallas_call x1, Pallas kernels, shards(): pl.pallas_call(kernel, out_shape=(jax.ShapeDtypeStruct((tok_dev, model),...  37 us
    pallas_call x1, Pallas kernels, shards(): pl.pallas_call(deliver, out_shape=tuple((jax.ShapeDtypeStruct(r.shape, r....  1.88 us

profile of v4, /device:TPU:0, one launch (start us, length us, event | category | flops | bytes accessed | tf_op | source)
XLA Modules:
  0.0 40.8 jit_solution(14312680545585733085)
XLA Ops:
  1.9 37.0 %shard_map.104 = (bf16[64,1536]{1,0:T(8,128)(2,1)}, bf16[2,128,768]{2,1,0:T(8,128)(2,1)}) custom-call(s32[1]{0:T(128)S(6)} %copy.11.refs_0_, s32[1]{0:T(128)S(6)} %copy.12.refs_1_, bf16[64,1536]{1,0:T(8,128)(2,1)} %refs_2_.1, f32[3,28,1536]{2,1,0:T(8,128)} %bitcast.5, bf16[3,1536,768]{2,1,0:T(8,128)(2,1)} %bitcast.4, f32[1,128]{1,0:T(1,128)} %bitcast.6, ...), custom_call_target="tpu_custom_call" | custom-call | tf_op jit(solution)/shard_map/pallas_call | solution.py:387
  38.9 1.9 %shard_map.105 = (bf16[64,1536]{1,0:T(8,128)(2,1)}, bf16[2,128,768]{2,1,0:T(8,128)(2,1)}) custom-call(bf16[64,1536]{1,0:T(8,128)(2,1)} %get-tuple-element.4.update, bf16[2,128,768]{2,1,0:T(8,128)(2,1)} %get-tuple-element.5.new_kv), custom_call_target="tpu_custom_call" | custom-call | tf_op jit(solution)/shard_map/pallas_call | solution.py:423
